TPU v7x, 256 devices: a whole 4x4x8 slice. The times are simulated.
256 devices in a mesh: rows: 32 (over z, y), cols: 8 (over x, core).
Axes of the slice: x: 4, y: 4, z: 8, core: 2. Of those that a mesh axis runs over, the one named last changes fastest.
Arguments:
- embedding: float32 [40960, 4096], P('rows', 'cols'), may hold values from -50 to 50
- test_matrix: float32 [4096, 640], P('cols'), may hold values from -0.09375 to 0.09375
Outputs:
- whitened: float32 [40960, 640], P(('rows', 'cols'))
- col_basis: float32 [4096, 640], P('cols')
All inputs are finite; a program needn't handle non-finite values.
Results may differ from a plain program's by a relative error of at most 0.000092.
Values sent between devices are 32-bit elements; how exact they have to be, the bound alone decides.
A program may use at most 64 MiB of HBM per device.

v0:
```python
import jax
import jax.numpy as jnp
from jax import lax
from jax.sharding import PartitionSpec as P

precise = lax.Precision.HIGHEST


def contract(left_mat, right_mat):
    return lax.dot_general(
        left_mat,
        right_mat,
        (((0,), (0,)), ((), ())),
        precision=precise,
        preferred_element_type=jnp.float32,
    )


def whiten(matrix, gram_full):
    lower_factor = jnp.linalg.cholesky(gram_full)
    return jax.scipy.linalg.solve_triangular(lower_factor, matrix.T, lower=True).T


def body(embedding, test_matrix):
    rows_local = embedding.shape[0]
    width_local = embedding.shape[1]
    col_count = lax.axis_size("cols")
    row_count = lax.axis_size("rows")
    share_rows = rows_local // col_count
    total_rows = rows_local * row_count
    total_width = width_local * col_count
    partial_sketch = jnp.dot(
        embedding, test_matrix, precision=precise, preferred_element_type=jnp.float32
    )
    sketch = lax.psum(partial_sketch, "cols")
    gram_full = lax.psum(contract(sketch, sketch), "rows") / total_rows
    whitened_all = whiten(sketch, gram_full)
    whitened = lax.dynamic_slice_in_dim(
        whitened_all, lax.axis_index("cols") * share_rows, share_rows, 0
    )
    dual_part = contract(embedding, whitened_all)
    dual_full = lax.psum(dual_part, "rows")
    dual_gram = lax.psum(contract(dual_full, dual_full), "cols") / total_width
    col_basis = whiten(dual_full, dual_gram)
    return (whitened, col_basis)


def solution(mesh):
    placed = (P("rows", "cols"), P("cols", None))
    return jax.shard_map(
        body,
        mesh=mesh,
        in_specs=placed,
        out_specs=(P(("rows", "cols"), None), P("cols", None)),
        check_vma=False,
    )
```

profile of v0, /device:TPU:65, one launch (start us, length us, event | category | flops | bytes accessed | tf_op | source)
XLA Modules:
  0.0 918.7 jit_solution(9898923368006869920)
XLA Ops:
  8.9 9.5 %fusion.92 = f32[1280,640]{1,0:T(8,128)} fusion(f32[1280,512]{1,0:T(8,128)S(1)} %copy-done, f32[512,640]{1,0:T(8,128)} %param.4), kind=kOutput, calls=%fused_computation.185 | convolution fusion | flops 5033164800 | bytes 7208960 | tf_op jit(solution)/shard_map/dot_general | solution.py:32
  19.0 74.6 %all-reduce.6.cloned.1.call-done = f32[1280,640]{1,0:T(8,128)} async-done(((f32[1280,640]{1,0:T(8,128)}), f32[1280,640]{1,0:T(8,128)}) %all-reduce.6.cloned.1.call-update) | async-done | bytes 3276816 | tf_op jit(solution)/shard_map/psum | solution.py:35
  93.6 12.3 %fusion.93 = f32[640,640]{0,1:T(8,128)} fusion(f32[1280,640]{1,0:T(8,128)} %all-reduce.6.cloned.1.call-done), kind=kOutput, calls=%fused_computation.186 | convolution fusion | flops 6291456000 | bytes 4915200 | tf_op jit(solution)/shard_map/dot_general | solution.py:10
  105.9 148.7 %all-reduce.8.cloned.1.call-done = f32[640,640]{0,1:T(8,128)} async-done(((f32[640,640]{0,1:T(8,128)}), f32[640,640]{0,1:T(8,128)}) %all-reduce.8.cloned.1.call-update) | async-done | bytes 1638416 | tf_op jit(solution)/shard_map/psum | solution.py:36
  254.6 2.7 broadcast_multiply_fusion.1
  257.4 2.9 copy.5
  263.6 11.7 %cholesky.364 = f32[128,128]{1,0:T(8,128)S(1)} custom-call(f32[128,128]{1,0:T(8,128)S(1)} %cholesky.542), custom_call_target="Cholesky" | custom-call | tf_op jit(solution)/shard_map/jit(cholesky)/cholesky | solution.py:20
  275.3 9.8 %custom-call.40 = f32[1,128,128]{1,2,0:T(8,128)S(1)} custom-call(f32[1,128,128]{2,1,0:T(8,128)S(1)} %get-tuple-element.66), custom_call_target="InvertDiagBlocksLowerTriangular" | custom-call | tf_op jit(solution)/shard_map/jit(cholesky)/cholesky | solution.py:20
  289.9 11.7 %cholesky.383 = f32[128,128]{1,0:T(8,128)S(1)} custom-call(f32[128,128]{1,0:T(8,128)S(1)} %cholesky.546), custom_call_target="Cholesky" | custom-call | tf_op jit(solution)/shard_map/jit(cholesky)/cholesky | solution.py:20
  302.2 10.0 %custom-call.41 = f32[1,128,128]{1,2,0:T(8,128)S(1)} custom-call(f32[1,128,128]{2,1,0:T(8,128)S(1)} %get-tuple-element.63), custom_call_target="InvertDiagBlocksLowerTriangular" | custom-call | tf_op jit(solution)/shard_map/jit(cholesky)/cholesky | solution.py:20
  314.8 11.7 %cholesky.404 = f32[128,128]{1,0:T(8,128)S(1)} custom-call(f32[128,128]{1,0:T(8,128)S(1)} %cholesky.551), custom_call_target="Cholesky" | custom-call | tf_op jit(solution)/shard_map/jit(cholesky)/cholesky | solution.py:20
  327.8 9.8 %custom-call.42 = f32[1,128,128]{1,2,0:T(8,128)S(1)} custom-call(f32[1,128,128]{2,1,0:T(8,128)S(1)} %get-tuple-element.60), custom_call_target="InvertDiagBlocksLowerTriangular" | custom-call | tf_op jit(solution)/shard_map/jit(cholesky)/cholesky | solution.py:20
  340.2 12.1 %cholesky.423 = f32[128,128]{1,0:T(8,128)S(1)} custom-call(f32[128,128]{1,0:T(8,128)S(1)} %cholesky.556), custom_call_target="Cholesky" | custom-call | tf_op jit(solution)/shard_map/jit(cholesky)/cholesky | solution.py:20
  353.6 9.8 %custom-call.43 = f32[1,128,128]{1,2,0:T(8,128)S(1)} custom-call(f32[1,128,128]{2,1,0:T(8,128)S(1)} %get-tuple-element.57), custom_call_target="InvertDiagBlocksLowerTriangular" | custom-call | tf_op jit(solution)/shard_map/jit(cholesky)/cholesky | solution.py:20
  365.7 11.7 %cholesky.440 = f32[128,128]{1,0:T(8,128)S(1)} custom-call(f32[128,128]{1,0:T(8,128)S(1)} %convolution_subtract_fusion.14), custom_call_target="Cholesky" | custom-call | tf_op jit(solution)/shard_map/jit(cholesky)/cholesky | solution.py:20
  382.5 2.7 select_select_fusion.1
  385.2 14.0 %while.2 = (s32[]{:T(128)}, f32[640,640]{1,0:T(8,128)}, s32[5,2]{0,1:T(2,128)S(1)}, f32[5,128,128]{2,1,0:T(8,128)S(1)}, s32[]{:T(128)}) while((s32[]{:T(128)}, f32[640,640]{1,0:T(8,128)}, s32[5,2]{0,1:T(2,128)S(1)}, f32[5,128,128]{2,1,0:T(8,128)S(1)}, s32[]{:T(128)}) %tuple.66), condition=%wide.while_cond, body=%wide.while_body.sunk | while | flops 2 | bytes 131181 | solution.py:21
  385.8 2.2 bitcast_dynamic-update-slice_fusion.4
  394.3 2.2 bitcast_dynamic-update-slice_fusion.4
  399.2 49.3 %custom-call.34 = f32[5,128,128]{1,2,0:T(8,128)S(1)} custom-call(f32[5,128,128]{2,1,0:T(8,128)S(1)} %get-tuple-element.10), custom_call_target="InvertDiagBlocksLowerTriangular" | custom-call | tf_op jit(solution)/shard_map/jit(_solve_triangular)/triangular_solve | solution.py:21
  450.4 2.5 convolution_subtract_fusion.2
  453.6 3.2 convolution_subtract_fusion.1
  457.5 4.4 convolution_subtract_fusion
  462.7 5.5 fusion.8
  470.7 6.4 convolution_bitcast_fusion
  477.2 147.6 %all-reduce.10.cloned.1.call-done = f32[512,640]{0,1:T(8,128)} async-done(((f32[512,640]{0,1:T(8,128)}), f32[512,640]{0,1:T(8,128)}) %all-reduce.10.cloned.1.call-update) | async-done | bytes 1310736 | tf_op jit(solution)/shard_map/psum | solution.py:42
  624.8 6.3 fusion.94
  633.5 67.8 %all-reduce.12.cloned.1.call-done = f32[640,640]{0,1:T(8,128)} async-done(((f32[640,640]{0,1:T(8,128)}), f32[640,640]{0,1:T(8,128)}) %all-reduce.12.cloned.1.call-update) | async-done | bytes 1638416 | tf_op jit(solution)/shard_map/psum | solution.py:43
  701.2 2.7 broadcast_multiply_fusion
  704.0 3.1 copy.7
  710.4 11.7 %cholesky.455 = f32[128,128]{1,0:T(8,128)S(1)} custom-call(f32[128,128]{1,0:T(8,128)S(1)} %cholesky.560), custom_call_target="Cholesky" | custom-call | tf_op jit(solution)/shard_map/jit(cholesky)/cholesky | solution.py:20
  723.4 9.8 %custom-call.44 = f32[1,128,128]{1,2,0:T(8,128)S(1)} custom-call(f32[1,128,128]{2,1,0:T(8,128)S(1)} %get-tuple-element.53), custom_call_target="InvertDiagBlocksLowerTriangular" | custom-call | tf_op jit(solution)/shard_map/jit(cholesky)/cholesky | solution.py:20
  736.6 11.7 %cholesky.474 = f32[128,128]{1,0:T(8,128)S(1)} custom-call(f32[128,128]{1,0:T(8,128)S(1)} %cholesky.564), custom_call_target="Cholesky" | custom-call | tf_op jit(solution)/shard_map/jit(cholesky)/cholesky | solution.py:20
  750.3 10.0 %custom-call.45 = f32[1,128,128]{1,2,0:T(8,128)S(1)} custom-call(f32[1,128,128]{2,1,0:T(8,128)S(1)} %get-tuple-element.50), custom_call_target="InvertDiagBlocksLowerTriangular" | custom-call | tf_op jit(solution)/shard_map/jit(cholesky)/cholesky | solution.py:20
  762.9 11.7 %cholesky.495 = f32[128,128]{1,0:T(8,128)S(1)} custom-call(f32[128,128]{1,0:T(8,128)S(1)} %cholesky.569), custom_call_target="Cholesky" | custom-call | tf_op jit(solution)/shard_map/jit(cholesky)/cholesky | solution.py:20
  775.9 9.8 %custom-call.46 = f32[1,128,128]{1,2,0:T(8,128)S(1)} custom-call(f32[1,128,128]{2,1,0:T(8,128)S(1)} %get-tuple-element.47), custom_call_target="InvertDiagBlocksLowerTriangular" | custom-call | tf_op jit(solution)/shard_map/jit(cholesky)/cholesky | solution.py:20
  788.3 11.9 %cholesky.514 = f32[128,128]{1,0:T(8,128)S(1)} custom-call(f32[128,128]{1,0:T(8,128)S(1)} %cholesky.574), custom_call_target="Cholesky" | custom-call | tf_op jit(solution)/shard_map/jit(cholesky)/cholesky | solution.py:20
  801.4 9.8 %custom-call.47 = f32[1,128,128]{1,2,0:T(8,128)S(1)} custom-call(f32[1,128,128]{2,1,0:T(8,128)S(1)} %get-tuple-element.44), custom_call_target="InvertDiagBlocksLowerTriangular" | custom-call | tf_op jit(solution)/shard_map/jit(cholesky)/cholesky | solution.py:20
  813.5 11.7 %cholesky.531 = f32[128,128]{1,0:T(8,128)S(1)} custom-call(f32[128,128]{1,0:T(8,128)S(1)} %convolution_subtract_fusion.13), custom_call_target="Cholesky" | custom-call | tf_op jit(solution)/shard_map/jit(cholesky)/cholesky | solution.py:20
  829.7 2.7 select_select_fusion
  832.5 14.6 %while.3 = (s32[]{:T(128)}, f32[640,640]{1,0:T(8,128)}, s32[5,2]{0,1:T(2,128)S(1)}, f32[5,128,128]{2,1,0:T(8,128)S(1)}, s32[]{:T(128)}) while((s32[]{:T(128)}, f32[640,640]{1,0:T(8,128)}, s32[5,2]{0,1:T(2,128)S(1)}, f32[5,128,128]{2,1,0:T(8,128)S(1)}, s32[]{:T(128)}) %tuple.80), condition=%wide.while_cond.1, body=%wide.while_body.1.sunk | while | flops 2 | bytes 131181 | solution.py:21
  833.1 2.3 bitcast_dynamic-update-slice_fusion.5
  836.1 2.3 bitcast_dynamic-update-slice_fusion.5
  839.0 2.3 bitcast_dynamic-update-slice_fusion.5
  841.9 2.3 bitcast_dynamic-update-slice_fusion.5
  844.9 2.2 bitcast_dynamic-update-slice_fusion.5
  847.1 49.4 %custom-call.35 = f32[5,128,128]{1,2,0:T(8,128)S(1)} custom-call(f32[5,128,128]{2,1,0:T(8,128)S(1)} %get-tuple-element.18), custom_call_target="InvertDiagBlocksLowerTriangular" | custom-call | tf_op jit(solution)/shard_map/jit(_solve_triangular)/triangular_solve | solution.py:21
  909.1 2.8 copy.9
  (110 shorter events, 78.7 us)
Async XLA Ops:
  7.2 1.7 copy-start
  7.2 86.4 %all-reduce.6.cloned.1.call-start = ((), (), s32[]{:S(2)}) async-start(), calls=%async_computation | async-start | bytes 6553600 | tf_op jit(solution)/shard_map/psum | solution.py:35
  18.4 236.2 %all-reduce.8.cloned.1.call-start = ((), (), s32[]{:S(2)}) async-start(), calls=%async_computation.1 | async-start | bytes 3276800 | tf_op jit(solution)/shard_map/psum | solution.py:36
  105.8 518.9 %all-reduce.10.cloned.1.call-start = ((), (), s32[]{:S(2)}) async-start(), calls=%async_computation.2 | async-start | bytes 2621440 | tf_op jit(solution)/shard_map/psum | solution.py:42
  262.4 1.2 copy-start.5
  450.4 3.3 copy-start.1
  469.0 1.7 copy-start.3
  477.1 224.1 %all-reduce.12.cloned.1.call-start = ((), (), s32[]{:S(2)}) async-start(), calls=%async_computation.3 | async-start | bytes 3276800 | tf_op jit(solution)/shard_map/psum | solution.py:43
  709.2 1.2 copy-start.4
  896.5 4.7 copy-start.2
Sparse Core Ops, SparseCore 0:
  18.5 74.9 all-reduce.5
  106.0 148.6 all-reduce.7
  477.2 147.4 all-reduce.9
  631.2 70.0 all-reduce.11
where the time goes:
time: 928 us; the launch traced here: 919 us
  waiting for transfers between devices  439 us (47%)
  other arithmetic  322 us (35%)
  matrix products  88.9 us (10%)
  local copies, waits for them, and re-layouts  48 us (5%)
  between operations  20.7 us (2%)
    another operation x37, other arithmetic, whiten(): lower_factor = jnp.linalg.cholesky(gram_full)  208 us
    psum x1, waiting for transfers between devices, body(): gram_full = lax.psum(contract(sketch, sketch), 'rows') / total_rows  149 us
    psum x1, waiting for transfers between devices, body(): dual_full = lax.psum(dual_part, 'rows')  148 us
    another operation x5, other arithmetic, whiten(): jax.scipy.linalg.solve_triangular(lower_factor, matrix.T, lower=True)  104 us
    psum x1, waiting for transfers between devices, body(): sketch = lax.psum(partial_sketch, 'cols')  74.6 us
    psum x1, waiting for transfers between devices, body(): dual_gram = lax.psum(contract(dual_full, dual_full), 'cols') / total_width  67.8 us
    another operation x18, matrix products, whiten(): jax.scipy.linalg.solve_triangular(lower_factor, matrix.T, lower=True)  33 us
    another operation x30, local copies, waits for them, and re-layouts  28.4 us
  transfers between devices with their start and end apart: 4, of which 4 were waited for; matrix products, arithmetic and copies ran while one was open for 0% of the time, Pallas kernels for 0%

commit v1 on v0

v1 whole, which is shorter than its diff:
```python
import jax
import jax.numpy as jnp
from jax import lax
from jax.experimental import pallas as pl
from jax.experimental.pallas import tpu as pltpu
from jax.sharding import PartitionSpec as P

precise = lax.Precision.HIGHEST
BLOCK = 128
TILE = 8
TILES = BLOCK // TILE


def dot(left_mat, right_mat, left_dim, right_dim):
    return lax.dot_general(
        left_mat,
        right_mat,
        (((left_dim,), (right_dim,)), ((), ())),
        precision=precise,
        preferred_element_type=jnp.float32,
    )


def invert_factor(rows):
    shape = (TILE, BLOCK)
    lane = lax.broadcasted_iota(jnp.int32, shape, 1)
    sub = lax.broadcasted_iota(jnp.int32, shape, 0)
    rows = list(rows)
    inverse = [
        jnp.where(lane == sub + TILE * i, 1.0, 0.0).astype(jnp.float32) for i in range(TILES)
    ]
    for tile in range(TILES):
        spread = {
            i: [
                jnp.broadcast_to(rows[i][:, col : col + 1], shape)
                for col in range(tile * TILE, tile * TILE + TILE)
            ]
            for i in range(tile, TILES)
        }
        pivots = None
        for t in range(TILE):
            pivot = jnp.broadcast_to(spread[tile][t][t : t + 1, :], shape)
            pivots = pivot if pivots is None else jnp.where(sub == t, pivot, pivots)
            inv_pivot = 1.0 / pivot
            pivot_cols = [
                jnp.broadcast_to(spread[tile][u][t : t + 1, :], shape) for u in range(t + 1, TILE)
            ]
            pivot_row = jnp.broadcast_to(rows[tile][t : t + 1, :], shape)
            pivot_inv = jnp.broadcast_to(inverse[tile][t : t + 1, :], shape)
            for i in range(tile, TILES):
                factor = spread[i][t] * inv_pivot
                if i == tile:
                    factor = jnp.where(sub > t, factor, 0.0)
                for u in range(t + 1, TILE):
                    spread[i][u] = spread[i][u] - factor * pivot_cols[u - t - 1]
                rows[i] = rows[i] - factor * pivot_row
                inverse[i] = inverse[i] - factor * pivot_inv
        inverse[tile] = inverse[tile] * lax.rsqrt(pivots)
    return jnp.concatenate(inverse, 0)


def whiten_kernel(gram_ref, mat_ref, out_ref, gram, mat):
    count = gram_ref.shape[0] // BLOCK
    gram[...] = gram_ref[...]
    mat[...] = mat_ref[...]
    for k in range(count):
        lo, hi = k * BLOCK, (k + 1) * BLOCK
        inverse = invert_factor([gram[lo + TILE * i : lo + TILE * (i + 1), lo:hi] for i in range(TILES)])
        done = dot(mat[:, lo:hi], inverse, 1, 1)
        out_ref[:, lo:hi] = done
        if k + 1 < count:
            below = dot(gram[hi:, lo:hi], inverse, 1, 1)
            gram[hi:, hi:] = gram[hi:, hi:] - dot(below, below, 1, 1)
            mat[:, hi:] = mat[:, hi:] - dot(done, below, 1, 1)


def whiten(matrix, gram_full):
    return pl.pallas_call(
        whiten_kernel,
        out_shape=jax.ShapeDtypeStruct(matrix.shape, jnp.float32),
        scratch_shapes=[
            pltpu.VMEM(gram_full.shape, jnp.float32),
            pltpu.VMEM(matrix.shape, jnp.float32),
        ],
        compiler_params=pltpu.CompilerParams(vmem_limit_bytes=40 * 2**20),
    )(gram_full, matrix)


def body(embedding, test_matrix):
    rows_local, width_local = embedding.shape
    col_count = lax.axis_size("cols")
    row_count = lax.axis_size("rows")
    share_rows = rows_local // col_count
    total_rows = rows_local * row_count
    total_width = width_local * col_count
    sketch = lax.psum(dot(embedding, test_matrix, 1, 0), "cols")
    gram_full = lax.psum(dot(sketch, sketch, 0, 0), "rows") / total_rows
    projected = lax.psum(dot(embedding, sketch, 0, 0), "rows")
    share = lax.dynamic_slice_in_dim(sketch, lax.axis_index("cols") * share_rows, share_rows, 0)
    both = whiten(jnp.concatenate([share, projected], 0), gram_full)
    whitened, dual_full = both[:share_rows], both[share_rows:]
    dual_gram = lax.psum(dot(dual_full, dual_full, 0, 0), "cols") / total_width
    return whitened, whiten(dual_full, dual_gram)


def solution(mesh):
    placed = (P("rows", "cols"), P("cols", None))
    return jax.shard_map(
        body,
        mesh=mesh,
        in_specs=placed,
        out_specs=(P(("rows", "cols"), None), P("cols", None)),
        check_vma=False,
    )
```

time: 928 us -> 415 us (0.45)
  other arithmetic: 322 us -> 3.43 us
  waiting for transfers between devices: 439 us -> 293 us
  matrix products: 88.9 us -> 34.3 us
  Pallas kernels: 0 us -> 52.8 us
  local copies, waits for them, and re-layouts: 48 us -> 8.48 us
    another operation x42 -> x0, other arithmetic: 312 us -> none  [the longest x37 208 us: whiten(): lower_factor = jnp.linalg.cholesky(gram_full)]
    psum x4 -> x3, waiting for transfers between devices: 439 us -> 293 us  [the longest x1 153 us: body(): gram_full = lax.psum(dot(sketch, sketch, 0, 0), 'rows') / total_rows]
    another operation x34 -> x0, matrix products: 54.5 us -> none  [the longest x18 33 us: whiten(): jax.scipy.linalg.solve_triangular(lower_factor, matrix.T, lower=True)]
    pallas_call x0 -> x2, Pallas kernels: none -> 52.8 us  [whiten(): pl.pallas_call(whiten_kernel, out_shape=jax.ShapeDtypeStruct(matrix.shape...]
    another operation x41 -> x0, local copies, waits for them, and re-layouts: 31 us -> none
  transfers between devices with their start and end apart: 4 -> 3, of which waited for: 4 -> 3; matrix products, arithmetic and copies ran while one was open for 0% -> 1% of each run, Pallas kernels for 0% -> 0%
where the time goes in v1:
time: 415 us; the launch traced here: 407 us
  waiting for transfers between devices  293 us (71%)
  Pallas kernels  52.8 us (13%)
  matrix products  34.3 us (8%)
  between operations  14.2 us (3%)
  local copies, waits for them, and re-layouts  8.48 us (2%)
    psum x1, waiting for transfers between devices, body(): gram_full = lax.psum(dot(sketch, sketch, 0, 0), 'rows') / total_rows  153 us
    psum x1, waiting for transfers between devices, body(): sketch = lax.psum(dot(embedding, test_matrix, 1, 0), 'cols')  74.9 us
    psum x1, waiting for transfers between devices, body(): dual_gram = lax.psum(dot(dual_full, dual_full, 0, 0), 'cols') / total_width  65.3 us
    pallas_call x2, Pallas kernels, whiten(): pl.pallas_call(whiten_kernel, out_shape=jax.ShapeDtypeStruct(matrix.shape...  52.8 us
    dot_general x4, matrix products, dot(): lax.dot_general(left_mat, right_mat, (((left_dim,), (right_dim,)), ((), (...  34.3 us
  transfers between devices with their start and end apart: 3, of which 3 were waited for; matrix products, arithmetic and copies ran while one was open for 1% of the time, Pallas kernels for 0%

profile of v1, /device:TPU:65, one launch (start us, length us, event | category | flops | bytes accessed | tf_op | source)
XLA Modules:
  0.0 407.0 jit_solution(8980309413921363515)
XLA Ops:
  7.2 0.0 copy-start
  7.2 0.0 all-reduce.5.cloned.1.call-start
  7.2 1.7 copy-done
  8.9 9.5 %fusion.2 = f32[1280,640]{1,0:T(8,128)} fusion(f32[1280,512]{1,0:T(8,128)S(1)} %copy-done, f32[512,640]{1,0:T(8,128)} %param.3), kind=kOutput, calls=%fused_computation.7 | convolution fusion | flops 5033164800 | bytes 7208960 | tf_op jit(solution)/shard_map/dot_general | solution.py:15
  18.4 0.0 all-reduce.5.cloned.1.call-update
  18.4 0.3 all-reduce.9.cloned.1.call-start
  18.7 74.9 %all-reduce.5.cloned.1.call-done = f32[1280,640]{1,0:T(8,128)} async-done(((f32[1280,640]{1,0:T(8,128)}), f32[1280,640]{1,0:T(8,128)}) %all-reduce.5.cloned.1.call-update) | async-done | bytes 3276816 | tf_op jit(solution)/shard_map/psum | solution.py:96
  93.5 0.0 copy-start.3
  93.5 9.7 %convolution_bitcast_fusion = f32[512,640]{1,0:T(8,128)} fusion(f32[1280,640]{1,0:T(8,128)} %all-reduce.5.cloned.1.call-done, f32[1280,512]{1,0:T(8,128)S(1)} %copy-done), kind=kOutput, calls=%fused_computation.1 | convolution fusion | flops 5033164800 | bytes 7208960 | tf_op jit(solution)/shard_map/dot_general | solution.py:15
  103.2 0.0 copy-done.3
  103.2 10.3 %fusion.3 = f32[640,640]{1,0:T(8,128)} fusion(f32[1280,640]{1,0:T(8,128)S(1)} %copy-done.3), kind=kOutput, calls=%fused_computation.8 | convolution fusion | flops 6291456000 | bytes 4915200 | tf_op jit(solution)/shard_map/dot_general | solution.py:15
  113.5 0.0 all-reduce.9.cloned.1.call-update
  113.6 0.0 all-reduce.7.cloned.1.call-start
  113.6 1.0 constant_dynamic-slice_fusion
  114.7 153.2 %all-reduce.9.cloned.1.call-done = (f32[640,640]{1,0:T(8,128)}, f32[512,640]{1,0:T(8,128)}) async-done(((f32[640,640]{1,0:T(8,128)}, f32[512,640]{1,0:T(8,128)}), (f32[640,640]{1,0:T(8,128)}, f32[512,640]{1,0:T(8,128)})) %all-reduce.9.cloned.1.call-update) | async-done | bytes 2949136 | tf_op jit(solution)/shard_map/psum | solution.py:97
  267.9 0.0 copy-start.4
  267.9 1.7 broadcast_multiply_fusion.1.gram_ref
  269.5 0.1 copy-done.4
  269.7 0.1 pad_maximum_fusion.mat_ref
  269.8 26.0 %shard_map.41 = f32[672,640]{1,0:T(8,128)S(1)} custom-call(f32[640,640]{1,0:T(8,128)S(1)} %broadcast_multiply_fusion.1.gram_ref, f32[672,640]{1,0:T(8,128)S(1)} %pad_maximum_fusion.mat_ref), custom_call_target="tpu_custom_call" | custom-call | tf_op jit(solution)/shard_map/pallas_call | solution.py:78
  295.8 0.0 copy-start.1
  295.9 1.2 copy-done.1
  297.1 4.9 %fusion = f32[640,640]{1,0:T(8,128)} fusion(f32[672,640]{1,0:T(8,128)S(1)} %shard_map.41), kind=kOutput, calls=%fused_computation.5 | convolution fusion | flops 2516582400 | bytes 2949120 | tf_op jit(solution)/shard_map/dot_general | solution.py:15
  301.9 0.0 all-reduce.7.cloned.1.call-update
  302.0 1.8 slice.8
  303.7 2.5 slice.9.mat_ref
  306.2 65.3 %all-reduce.7.cloned.1.call-done = f32[640,640]{1,0:T(8,128)} async-done(((f32[640,640]{1,0:T(8,128)}), f32[640,640]{1,0:T(8,128)}) %all-reduce.7.cloned.1.call-update) | async-done | bytes 1638416 | tf_op jit(solution)/shard_map/psum | solution.py:102
  371.5 0.0 copy-start.2
  371.5 1.6 broadcast_multiply_fusion.gram_ref
  373.1 0.2 copy-done.2
  373.3 26.8 %shard_map.42 = f32[512,640]{1,0:T(8,128)} custom-call(f32[640,640]{1,0:T(8,128)S(1)} %broadcast_multiply_fusion.gram_ref, f32[512,640]{1,0:T(8,128)S(1)} %copy-done.2), custom_call_target="tpu_custom_call" | custom-call | tf_op jit(solution)/shard_map/pallas_call | solution.py:78
Async XLA Ops:
  7.2 1.7 copy-start
  7.2 86.4 %all-reduce.5.cloned.1.call-start = ((), (), s32[]{:S(2)}) async-start(), calls=%async_computation | async-start | bytes 6553600 | tf_op jit(solution)/shard_map/psum | solution.py:96
  18.4 249.5 %all-reduce.9.cloned.1.call-start = ((), (), s32[]{:S(2)}) async-start(), calls=%async_computation.2 | async-start | bytes 5898240 | tf_op jit(solution)/shard_map/psum | solution.py:97
  93.5 9.7 %copy-start.3 = (f32[1280,640]{1,0:T(8,128)S(1)}, f32[1280,640]{1,0:T(8,128)}, u32[]{:S(2)}) copy-start(f32[1280,640]{1,0:T(8,128)} %all-reduce.5.cloned.1.call-done) | copy-start | bytes 9830404
  113.6 257.9 %all-reduce.7.cloned.1.call-start = ((), (), s32[]{:S(2)}) async-start(), calls=%async_computation.1 | async-start | bytes 3276800 | tf_op jit(solution)/shard_map/psum | solution.py:102
  267.9 1.8 copy-start.4
  295.8 1.2 copy-start.1
  371.5 1.8 copy-start.2
Sparse Core Ops, SparseCore 0:
  18.5 74.9 all-reduce.4
  113.7 154.1 all-reduce.8
  302.1 69.3 all-reduce.6

commit v2 on v1

--- a/solution.py
+++ b/solution.py
@@ -1,3 +1,5 @@
+import functools
+
 import jax
 import jax.numpy as jnp
 from jax import lax
@@ -59,48 +61,406 @@
     return jnp.concatenate(inverse, 0)
 
 
-def whiten_kernel(gram_ref, mat_ref, out_ref, gram, mat):
-    count = gram_ref.shape[0] // BLOCK
-    gram[...] = gram_ref[...]
-    mat[...] = mat_ref[...]
-    for k in range(count):
-        lo, hi = k * BLOCK, (k + 1) * BLOCK
+XS, YS, ZS = 4, 4, 8
+VMEM_LIMIT = 56 * 2**20
+
+
+def device(z, y, x, k):
+    return {"rows": z * YS + y, "cols": x * 2 + k}
+
+
+def place():
+    r, c = lax.axis_index("rows"), lax.axis_index("cols")
+    return r // YS, r % YS, c // 2, c % 2
+
+
+def along(axis, here, d):
+    z, y, x, k = here
+    if axis == "z":
+        return device((z + d) % ZS, y, x, k)
+    if axis == "y":
+        return device(z, (y + d) % YS, x, k)
+    if axis == "x":
+        return device(z, y, (x + d) % XS, k)
+    return device(z, y, x, 1 - k)
+
+
+SIZE = {"z": ZS, "y": YS, "x": XS, "k": 2}
+
+
+def enter(axes, here):
+    barrier = pltpu.get_barrier_semaphore()
+    count = 0
+    for axis in axes:
+        for d in range(1, SIZE[axis]):
+            pl.semaphore_signal(
+                barrier, inc=1, device_id=along(axis, here, d), device_id_type=pl.DeviceIdType.MESH
+            )
+            count += 1
+    return barrier, count
+
+
+def send(src, dst, sems, slot, to):
+    copy = pltpu.make_async_remote_copy(
+        src_ref=src,
+        dst_ref=dst,
+        send_sem=sems.at[0, slot],
+        recv_sem=sems.at[1, slot],
+        device_id=to,
+        device_id_type=pl.DeviceIdType.MESH,
+    )
+    copy.start()
+    return copy
+
+
+def scatter(axis, here, src, rows, landing, sems):
+    pos = here["zyxk".index(axis)]
+    return [
+        send(
+            src.at[pl.ds(((pos + d) % SIZE[axis]) * rows, rows)],
+            landing.at[d - 1],
+            sems,
+            d - 1,
+            along(axis, here, d),
+        )
+        for d in range(1, SIZE[axis])
+    ]
+
+
+def gather(axis, here, buf, first, rows, sems):
+    return [
+        send(
+            buf.at[pl.ds(first, rows)], buf.at[pl.ds(first, rows)], sems, d - 1, along(axis, here, d)
+        )
+        for d in range(1, SIZE[axis])
+    ]
+
+
+def wait(copies):
+    for copy in copies:
+        copy.wait()
+
+
+def total(first, landing):
+    value = first
+    for d in range(landing.shape[0]):
+        value = value + landing[d]
+    return value
+
+
+def slots_of(mat, out):
+    for i in range(5):
+        lo = i * BLOCK
+        strip = dot(mat[:, lo : lo + BLOCK], mat[:, : lo + BLOCK], 0, 0)
+        for j in range(i + 1):
+            slot = i * (i + 1) // 2 + j
+            out[slot // 8, pl.ds((slot % 8) * BLOCK, BLOCK), :] = strip[:, j * BLOCK : (j + 1) * BLOCK]
+    out[1, pl.ds(7 * BLOCK, BLOCK), :] = jnp.zeros((BLOCK, BLOCK), jnp.float32)
+
+
+def sum_gram(here, part, sums, landings, sems, out):
+    z, y, x, k = here
+    by_k, by_y, by_z, by_x = landings
+    sum_y, sum_z = sums
+    rows_y, rows_z = 1024 // YS, 1024 // YS // ZS
+    copy = send(part.at[1 - k], by_k, sems["k"], 0, along("k", here, 1))
+    yield
+    copy.wait()
+    part[k] = part[k] + by_k[...]
+    copies = scatter("y", here, part.at[k], rows_y, by_y, sems["y"])
+    yield
+    wait(copies)
+    sum_y[...] = total(part[k, pl.ds(y * rows_y, rows_y), :], by_y)
+    copies = scatter("z", here, sum_y, rows_z, by_z, sems["z"])
+    yield
+    wait(copies)
+    by_x[x] = total(sum_y[pl.ds(z * rows_z, rows_z), :], by_z)
+    copies = [
+        send(by_x.at[x], by_x.at[x], sems["x"], d - 1, along("x", here, d)) for d in range(1, XS)
+    ]
+    yield
+    wait(copies)
+    first = y * rows_y + z * rows_z
+    out[k, pl.ds(first, rows_z), :] = (by_x[0] + by_x[1]) + (by_x[2] + by_x[3])
+    copies = gather("z", here, out.at[k], first, rows_z, sems["gz"])
+    yield
+    wait(copies)
+    copies = gather("y", here, out.at[k], y * rows_y, rows_y, sems["gy"])
+    yield
+    wait(copies)
+    copy = send(out.at[k], out.at[k], sems["gk"], 0, along("k", here, 1))
+    yield
+    copy.wait()
+
+
+def sum_rows(here, order, part, sum_first, landings, sems, out):
+    at = {"z": here[0], "y": here[1]}
+    first, second = order
+    rows_first = part.shape[0] // SIZE[first]
+    rows_second = rows_first // SIZE[second]
+    copies = scatter(first, here, part, rows_first, landings[0], sems[0])
+    yield
+    wait(copies)
+    sum_first[...] = total(part[pl.ds(at[first] * rows_first, rows_first), :], landings[0])
+    copies = scatter(second, here, sum_first, rows_second, landings[1], sems[1])
+    yield
+    wait(copies)
+    mine = at[first] * rows_first + at[second] * rows_second
+    out[pl.ds(mine, rows_second), :] = total(
+        sum_first[pl.ds(at[second] * rows_second, rows_second), :], landings[1]
+    )
+    copies = gather(second, here, out, mine, rows_second, sems[2])
+    yield
+    wait(copies)
+    copies = gather(first, here, out, at[first] * rows_first, rows_first, sems[3])
+    yield
+    wait(copies)
+
+
+def sketch_kernel(
+    emb_hbm, test_hbm,
+    share_ref, proj_a_ref, proj_b_ref, gram_ref,
+    emb, test, load_sems,
+    part, by_core, by_x, core_sems, x_sems,
+    slab, gx_sems, gcore_sems,
+    proj_a, proj_b,
+    a_sum, a_in0, a_in1, a_s0, a_s1, a_s2, a_s3,
+    b_sum, b_in0, b_in1, b_s0, b_s1, b_s2, b_s3,
+    gram_part, sum_y, sum_z, g_k, g_y, g_z, g_x, gs_k, gs_y, gs_z, gs_x, gs_gz, gs_gy, gs_gk,
+):
+    here = place()
+    z, y, x, k = here
+    me = x * 2 + k
+    share = part.shape[2]
+    barrier, count = enter("kxyz", here)
+    load_test = pltpu.make_async_copy(test_hbm, test, load_sems.at[0])
+    load_emb = pltpu.make_async_copy(emb_hbm, emb, load_sems.at[1])
+    load_test.start()
+    load_emb.start()
+    load_test.wait()
+    load_emb.wait()
+
+    order = (2, 1, 3, 0)
+    core_copies, x_copies = [], []
+
+    def hand_on(step):
+        core_copies[step].wait()
+        part[step, k] = part[step, k] + by_core[step]
+        d = order[step]
+        if d:
+            x_copies.append(send(part.at[step, k], by_x.at[d - 1], x_sems, d - 1, along("x", here, d)))
+
+    for step, d in enumerate(order):
+        target = (x + d) % XS
+
+        @pl.loop(0, 2)
+        def _(half):
+            first = pl.multiple_of((target * 2 + half) * share, share)
+            part[step, half] = dot(emb[pl.ds(first, share), :], test[...], 1, 0)
+
+        if step == 0:
+            pl.semaphore_wait(barrier, count)
+        core_copies.append(
+            send(part.at[step, 1 - k], by_core.at[step], core_sems, step, along("k", here, 1))
+        )
+        if step:
+            hand_on(step - 1)
+    hand_on(3)
+    wait(x_copies)
+    slab[me] = total(part[3, k], by_x)
+
+    x_gather = {
+        d: send(slab.at[me], slab.at[me], gx_sems, d - 1, along("x", here, d)) for d in (2, 1, 3)
+    }
+    core_gather = {0: send(slab.at[me], slab.at[me], gcore_sems, 0, along("k", here, 1))}
+    share_ref[...] = slab[me]
+
+    slots_of(share_ref, gram_part)
+    gram_sum = sum_gram(
+        here, gram_part, (sum_y, sum_z), (g_k, g_y, g_z, g_x),
+        dict(k=gs_k, y=gs_y, z=gs_z, x=gs_x, gz=gs_gz, gy=gs_gy, gk=gs_gk), gram_ref,
+    )
+    next(gram_sum, None)
+
+    def project(d):
+        source = (x + XS - d) % XS
+        core_gather[d].wait()
+        for half in range(2):
+            one = slab.at[source * 2 + half]
+            rows = emb[pl.ds(pl.multiple_of((source * 2 + half) * share, share), share), :]
+            for into, lo, hi in ((proj_a, 0, 384), (proj_b, 384, 640)):
+                value = dot(rows, one[:, lo:hi], 0, 0)
+                if d == 0 and half == 0:
+                    into[...] = value
+                else:
+                    into[...] = into[...] + value
+
+    def forward(d):
+        x_gather[d].wait()
+        source = (x + XS - d) % XS
+        core_gather[d] = send(
+            slab.at[source * 2 + k], slab.at[source * 2 + k], gcore_sems, d, along("k", here, 1)
+        )
+
+    next(gram_sum, None)
+    project(0)
+    forward(1)
+    next(gram_sum, None)
+    project(1)
+    forward(3)
+    project(3)
+    next(gram_sum, None)
+    forward(2)
+    project(2)
+    sum_a = sum_rows(here, "yz", proj_a, a_sum, (a_in0, a_in1), (a_s0, a_s1, a_s2, a_s3), proj_a_ref)
+    sum_b = sum_rows(here, "zy", proj_b, b_sum, (b_in0, b_in1), (b_s0, b_s1, b_s2, b_s3), proj_b_ref)
+    next(sum_a, None)
+    next(sum_b, None)
+    next(gram_sum, None)
+    next(gram_sum, None)
+    next(gram_sum, None)
+    next(gram_sum, None)
+    for _ in range(4):
+        next(sum_a, None)
+        next(sum_b, None)
+
+
+def dma(*shape):
+    return pltpu.SemaphoreType.DMA(shape)
+
+
+def vmem(*shape):
+    return pltpu.VMEM(shape, jnp.float32)
+
+
+def pair(n):
+    return dma(2, n)
+
+
+def sketch_step(embedding, test_matrix):
+    rows, width = embedding.shape
+    rank = test_matrix.shape[1]
+    share = rows // 8
+    a, b = 384, rank - 384
+    f32 = lambda *shape: jax.ShapeDtypeStruct(shape, jnp.float32)
+    scratch = [vmem(rows, width), vmem(width, rank), dma(2)]
+    scratch += [vmem(4, 2, share, rank), vmem(4, share, rank), vmem(3, share, rank), pair(4), pair(3)]
+    scratch += [vmem(8, share, rank), pair(3), pair(4)]
+    scratch += [vmem(width, a), vmem(width, b)]
+    scratch += [vmem(width // 4, a), vmem(3, width // 4, a), vmem(7, width // 32, a)]
+    scratch += [pair(3), pair(7), pair(7), pair(3)]
+    scratch += [vmem(width // 8, b), vmem(7, width // 8, b), vmem(3, width // 32, b)]
+    scratch += [pair(7), pair(3), pair(3), pair(7)]
+    scratch += [vmem(2, 1024, 128), vmem(256, 128), vmem(32, 128)]
+    scratch += [vmem(1024, 128), vmem(3, 256, 128), vmem(7, 32, 128), vmem(4, 32, 128)]
+    scratch += [pair(1), pair(3), pair(7), pair(3), pair(7), pair(3), pair(1)]
+    return pl.pallas_call(
+        sketch_kernel,
+        out_shape=(f32(share, rank), f32(width, a), f32(width, b), f32(2, 1024, 128)),
+        in_specs=[pl.BlockSpec(memory_space=pl.ANY)] * 2,
+        out_specs=[pl.BlockSpec(memory_space=pltpu.VMEM)] * 4,
+        scratch_shapes=scratch,
+        name="sketch_step",
+        compiler_params=pltpu.CompilerParams(
+            collective_id=0, has_side_effects=True, vmem_limit_bytes=VMEM_LIMIT
+        ),
+    )(embedding, test_matrix)
+
+
+def cols_kernel(part_ref, out_ref, part, by_k, by_x, s_k, s_x, s_gx, s_gk):
+    here = place()
+    z, y, x, k = here
+    barrier, count = enter("kx", here)
+    part[...] = part_ref[...]
+    pl.semaphore_wait(barrier, count)
+    send(part.at[1 - k], by_k, s_k, 0, along("k", here, 1)).wait()
+    part[k] = part[k] + by_k[...]
+    wait(scatter("x", here, part.at[k], 256, by_x, s_x))
+    out_ref[k, pl.ds(x * 256, 256), :] = total(part[k, pl.ds(x * 256, 256), :], by_x)
+    wait(gather("x", here, out_ref.at[k], x * 256, 256, s_gx))
+    send(out_ref.at[k], out_ref.at[k], s_gk, 0, along("k", here, 1)).wait()
+
+
+def sum_over_cols(slots):
+    return pl.pallas_call(
+        cols_kernel,
+        out_shape=jax.ShapeDtypeStruct(slots.shape, jnp.float32),
+        in_specs=[pl.BlockSpec(memory_space=pltpu.VMEM)],
+        out_specs=pl.BlockSpec(memory_space=pltpu.VMEM),
+        scratch_shapes=[
+            vmem(2, 1024, 128), vmem(1024, 128), vmem(3, 256, 128), pair(1), pair(3), pair(3), pair(1)
+        ],
+        name="sum_over_cols",
+        compiler_params=pltpu.CompilerParams(
+            collective_id=1, has_side_effects=True, vmem_limit_bytes=VMEM_LIMIT
+        ),
+    )(slots)
+
+
+def load_gram(slots_ref, gram, scale):
+    for i in range(5):
+        for j in range(i + 1):
+            slot = i * (i + 1) // 2 + j
+            block = slots_ref[slot // 8, pl.ds((slot % 8) * BLOCK, BLOCK), :]
+            gram[pl.ds(i * BLOCK, BLOCK), pl.ds(j * BLOCK, BLOCK)] = block * scale
+
+
+def factor_and_apply(gram, mats):
+    count = gram.shape[0] // BLOCK
+    for step in range(count):
+        lo, hi = step * BLOCK, (step + 1) * BLOCK
         inverse = invert_factor([gram[lo + TILE * i : lo + TILE * (i + 1), lo:hi] for i in range(TILES)])
-        done = dot(mat[:, lo:hi], inverse, 1, 1)
-        out_ref[:, lo:hi] = done
-        if k + 1 < count:
+        if hi < gram.shape[0]:
             below = dot(gram[hi:, lo:hi], inverse, 1, 1)
-            gram[hi:, hi:] = gram[hi:, hi:] - dot(below, below, 1, 1)
-            mat[:, hi:] = mat[:, hi:] - dot(done, below, 1, 1)
-
-
-def whiten(matrix, gram_full):
-    return pl.pallas_call(
-        whiten_kernel,
-        out_shape=jax.ShapeDtypeStruct(matrix.shape, jnp.float32),
-        scratch_shapes=[
-            pltpu.VMEM(gram_full.shape, jnp.float32),
-            pltpu.VMEM(matrix.shape, jnp.float32),
-        ],
-        compiler_params=pltpu.CompilerParams(vmem_limit_bytes=40 * 2**20),
-    )(gram_full, matrix)
+            for left in range(hi, gram.shape[0], BLOCK):
+                gram[left:, left : left + BLOCK] = gram[left:, left : left + BLOCK] - dot(
+                    below[left - hi :], below[left - hi : left - hi + BLOCK], 1, 1
+                )
+        for mat in mats:
+            done = dot(mat[:, lo:hi], inverse, 1, 1)
+            mat[:, lo:hi] = done
+            if hi < gram.shape[0]:
+                mat[:, hi:] = mat[:, hi:] - dot(done, below, 1, 1)
+
+
+def first_kernel(scale, slots_ref, share_ref, proj_a_ref, proj_b_ref, white_ref, dual_ref, out_ref, gram):
+    load_gram(slots_ref, gram, scale)
+    white_ref[...] = share_ref[...]
+    dual_ref[:, :384] = proj_a_ref[...]
+    dual_ref[:, 384:] = proj_b_ref[...]
+    factor_and_apply(gram, (white_ref, dual_ref))
+    slots_of(dual_ref, out_ref)
+
+
+def second_kernel(scale, slots_ref, dual_ref, out_ref, gram):
+    load_gram(slots_ref, gram, scale)
+    out_ref[...] = dual_ref[...]
+    factor_and_apply(gram, (out_ref,))
 
 
 def body(embedding, test_matrix):
     rows_local, width_local = embedding.shape
-    col_count = lax.axis_size("cols")
-    row_count = lax.axis_size("rows")
-    share_rows = rows_local // col_count
-    total_rows = rows_local * row_count
-    total_width = width_local * col_count
-    sketch = lax.psum(dot(embedding, test_matrix, 1, 0), "cols")
-    gram_full = lax.psum(dot(sketch, sketch, 0, 0), "rows") / total_rows
-    projected = lax.psum(dot(embedding, sketch, 0, 0), "rows")
-    share = lax.dynamic_slice_in_dim(sketch, lax.axis_index("cols") * share_rows, share_rows, 0)
-    both = whiten(jnp.concatenate([share, projected], 0), gram_full)
-    whitened, dual_full = both[:share_rows], both[share_rows:]
-    dual_gram = lax.psum(dot(dual_full, dual_full, 0, 0), "cols") / total_width
-    return whitened, whiten(dual_full, dual_gram)
+    total_rows = rows_local * lax.axis_size("rows")
+    total_width = width_local * lax.axis_size("cols")
+    rank = test_matrix.shape[1]
+    f32 = lambda *shape: jax.ShapeDtypeStruct(shape, jnp.float32)
+    params = pltpu.CompilerParams(vmem_limit_bytes=VMEM_LIMIT)
+    share, proj_a, proj_b, slots = sketch_step(embedding, test_matrix)
+    whitened, dual, dual_slots = pl.pallas_call(
+        functools.partial(first_kernel, 1.0 / total_rows),
+        out_shape=(f32(*share.shape), f32(width_local, rank), f32(2, 1024, 128)),
+        scratch_shapes=[vmem(rank, rank)],
+        name="whiten_sketch",
+        compiler_params=params,
+    )(slots, share, proj_a, proj_b)
+    col_basis = pl.pallas_call(
+        functools.partial(second_kernel, 1.0 / total_width),
+        out_shape=f32(width_local, rank),
+        scratch_shapes=[vmem(rank, rank)],
+        name="whiten_dual",
+        compiler_params=params,
+    )(sum_over_cols(dual_slots), dual)
+    return whitened, col_basis
 
 
 def solution(mesh):

time: 415 us -> 211 us (0.51); the launches traced: 407 us -> 207 us
  waiting for transfers between devices: 293 us -> 0 us
  Pallas kernels: 52.8 us -> 206 us
  matrix products: 34.3 us -> 0 us
  between operations: 14.2 us -> 1.09 us
  local copies, waits for them, and re-layouts: 8.48 us -> 0 us
    psum x3 -> x0, waiting for transfers between devices: 293 us -> none  [the longest x1 153 us: body(): gram_full = lax.psum(dot(sketch, sketch, 0, 0), 'rows') / total_rows]
    pallas_call x2 -> x4, Pallas kernels: 52.8 us -> 206 us  [the longest x1 124 us: sketch_step(): pl.pallas_call(sketch_kernel, out_shape=(f32(share, rank), f32(width, a),...]
    dot_general x4 -> x0, matrix products: 34.3 us -> none  [dot(): lax.dot_general(left_mat, right_mat, (((left_dim,), (right_dim,)), ((), (...]
    slice x2 -> x0, local copies, waits for them, and re-layouts: 4.24 us -> none  [body(): whitened, dual_full = (both[:share_rows], both[share_rows:])]
  transfers between devices with their start and end apart: 3 -> 0, of which waited for: 3 -> 0; matrix products, arithmetic and copies ran while one was open for 1% -> 0% of each run, Pallas kernels for 0% -> 0%
where the time goes in v2:
time: 211 us; the launch traced here: 207 us
  Pallas kernels  206 us (98%)
    pallas_call x1, Pallas kernels, sketch_step(): pl.pallas_call(sketch_kernel, out_shape=(f32(share, rank), f32(width, a),...  124 us
    pallas_call x1, Pallas kernels, body(): pl.pallas_call(functools.partial(first_kernel, 1.0 / total_rows), out_sha...  29.5 us
    pallas_call x1, Pallas kernels, body(): pl.pallas_call(functools.partial(second_kernel, 1.0 / total_width), out_s...  27.3 us
    pallas_call x1, Pallas kernels, sum_over_cols(): pl.pallas_call(cols_kernel, out_shape=jax.ShapeDtypeStruct(slots.shape, j...  25.9 us

profile of v2, /device:TPU:65, one launch (start us, length us, event | category | flops | bytes accessed | tf_op | source)
XLA Modules:
  0.0 207.3 jit_solution(7667103086973194881)
XLA Ops:
  0.6 123.6 %sketch_step.1 = (f32[160,640]{1,0:T(8,128)}, f32[512,384]{1,0:T(8,128)}, f32[512,256]{1,0:T(8,128)}, f32[2,1024,128]{2,1,0:T(8,128)}) custom-call(f32[1280,512]{1,0:T(8,128)} %emb_hbm.1, f32[512,640]{1,0:T(8,128)} %test_hbm.1), custom_call_target="tpu_custom_call" | custom-call | tf_op jit(solution)/shard_map/sketch_step/pallas_call | solution.py:357
  124.2 29.5 %whiten_sketch.1 = (f32[160,640]{1,0:T(8,128)}, f32[512,640]{1,0:T(8,128)}, f32[2,1024,128]{2,1,0:T(8,128)}) custom-call(f32[2,1024,128]{2,1,0:T(8,128)} %get-tuple-element.9.slots_ref, f32[160,640]{1,0:T(8,128)} %get-tuple-element.10.share_ref, f32[512,384]{1,0:T(8,128)} %get-tuple-element.11.proj_a_ref, f32[512,256]{1,0:T(8,128)} %get-tuple-element.12.proj_b_ref), custom_call_target="tpu_custom_call" | custom-call | tf_op jit(solution)/shard_map/whiten_sketch/pallas_call | solution.py:449
  153.7 25.9 %sum_over_cols.1.slots_ref = f32[2,1024,128]{2,1,0:T(8,128)} custom-call(f32[2,1024,128]{2,1,0:T(8,128)} %get-tuple-element.14.part_ref), custom_call_target="tpu_custom_call" | custom-call | tf_op jit(solution)/shard_map/sum_over_cols/pallas_call | solution.py:385
  179.5 27.3 %whiten_dual.1 = f32[512,640]{1,0:T(8,128)} custom-call(f32[2,1024,128]{2,1,0:T(8,128)} %sum_over_cols.1.slots_ref, f32[512,640]{1,0:T(8,128)} %get-tuple-element.15.dual_ref), custom_call_target="tpu_custom_call" | custom-call | tf_op jit(solution)/shard_map/whiten_dual/pallas_call | solution.py:456
